TPU v7x, 128 devices: a whole 4x4x4 slice. The times are simulated.
128 devices in a mesh: set: 16 (over x, z), lev: 8 (over y, core).
Axes of the slice: x: 4, y: 4, z: 4, core: 2. Of those that a mesh axis runs over, the one named last changes fastest.
Arguments:
- spectral: bfloat16 [2, 128, 2, 640, 1281], P(None, None, None, ('set', 'lev')), may hold values from -0.0048828125 to 0.0048828125
- vertical: bfloat16 [2, 128, 128], P(None, 'lev'), may hold values from -0.5 to 0.5
- value_table: bfloat16 [640, 1281, 128], P(('set', 'lev')), may hold values from -6 to 6
- slope_table: bfloat16 [640, 1281, 128], P(('set', 'lev')), may hold values from -6 to 6
- wave_low: int32 [640], P(('set', 'lev')), may hold values from 0 to 639, each once
- lat_slot: int32 [128], replicated, may hold values from 0 to 127, each once
- lon_counts: int32 [128], replicated, may hold values from 20 to 5136, as said below
Outputs:
- fields: bfloat16 [2, 128, 128, 1024], P(None, 'lev', 'set')
- slopes: bfloat16 [2, 128, 128, 1024], P(None, 'lev', 'set')
Inputs may be any that keep to these rules, and one draw needn't show every extreme that they name: `wave_low`: A permutation; pair slot p holds zonal wavenumbers wave_low[p] and 1279 - wave_low[p], so every wavenumber from 0 to 1279 appears once. `lat_slot`: A permutation of the window's latitudes. `lon_counts`: each count is 4 i + 16 for an octahedral latitude number i from 1 to 1280; the largest count is reached in every draw.
All inputs are finite; a program needn't handle non-finite values.
Results may differ from a plain program's by a relative error of at most 0.0062.
Values may be sent and summed in bfloat16 or wider, within the bound.
A program may use at most 128 MiB of HBM per device.

v0:
```python
import jax
import jax.numpy as jnp
from jax import lax
from jax.sharding import PartitionSpec as P

LONS = 1024


two_pi = 6.283185307179586


def degree_scale(low_waves, top_degree, pair_rows):
    column = jnp.arange(pair_rows, dtype=jnp.int32)
    is_low = column[None, :] <= (top_degree - low_waves)[:, None]
    degree = jnp.where(is_low, low_waves[:, None] + column[None, :], column[None, :] - 1)
    implicit_scale = (degree * (degree + 1)).astype(jnp.float32) / jnp.float32(
        top_degree * (top_degree + 1)
    )
    return (is_low, implicit_scale)


def longitude_table(wavenumbers, lon_count, columns):
    column = jnp.arange(columns, dtype=jnp.int32)
    product = wavenumbers[:, None] * column[None, :] % lon_count
    phase_angle = product.astype(jnp.float32) * (two_pi / lon_count.astype(jnp.float32))
    weight = jnp.where(wavenumbers == 0, 1.0, 2.0).astype(jnp.float32)[:, None]
    inside = (column < lon_count)[None, :]
    cosine = jnp.where(inside, weight * jnp.cos(phase_angle), 0.0)
    sine_part = jnp.where(inside, -weight * jnp.sin(phase_angle), 0.0)
    return jnp.concatenate([cosine, sine_part], axis=0).astype(jnp.bfloat16)


def body(spectral, vertical, value_table, slope_table, wave_low, lat_slot, lon_counts):
    levels_all = spectral.shape[1]
    pairs_local = spectral.shape[3]
    pair_rows = spectral.shape[4]
    top_degree = pair_rows - 2
    lat_total = value_table.shape[2]
    set_count = lax.axis_size("set")
    lev_count = lax.axis_size("lev")
    lev_local = levels_all // lev_count
    lat_local = lat_total // set_count
    matrices = lax.all_gather(vertical, "lev", axis=1, tiled=True)
    all_lows = lax.all_gather(wave_low, ("set", "lev"), axis=0, tiled=True)
    is_low, implicit_scale = degree_scale(wave_low, top_degree, pair_rows)
    coupled = jnp.einsum("flk,fkrpj->flrpj", matrices, spectral, preferred_element_type=jnp.float32)
    adjusted = (spectral.astype(jnp.float32) + implicit_scale * coupled).astype(jnp.bfloat16)
    low_keep = is_low.astype(jnp.bfloat16)
    high_keep = jnp.logical_not(is_low).astype(jnp.bfloat16)
    halves = jnp.stack([adjusted * low_keep, adjusted * high_keep])
    band_value = jnp.einsum(
        "hflrpj,pjq->hflrpq", halves, value_table, preferred_element_type=jnp.float32
    ).astype(jnp.bfloat16)
    band_slope = jnp.einsum(
        "hflrpj,pjq->hflrpq", halves, slope_table, preferred_element_type=jnp.float32
    ).astype(jnp.bfloat16)
    band_all = jnp.stack([band_value, band_slope])
    band_all = jnp.take(band_all, lat_slot, axis=6)
    band_all = band_all.reshape(2, 2, 2, lev_count, lev_local, 2, pairs_local, set_count, lat_local)
    outgoing = jnp.transpose(band_all, (7, 3, 2, 0, 4, 5, 8, 6, 1))
    inner_shape = outgoing.shape[2:]
    flat_out = outgoing.reshape((set_count * lev_count,) + inner_shape)
    incoming = lax.all_to_all(flat_out, ("set", "lev"), split_axis=0, concat_axis=0, tiled=True)
    rows_by_slot = jnp.transpose(incoming, (5, 1, 2, 3, 4, 0, 6, 7))
    rows_by_slot = rows_by_slot.reshape(lat_local, 4 * lev_local, 2 * (top_degree + 1))
    wavenumbers = jnp.stack([all_lows, top_degree - all_lows], axis=-1).reshape(-1)
    slot_numbers = lax.axis_index("set") * lat_local + jnp.arange(lat_local, dtype=jnp.int32)
    latitudes = jnp.take(lat_slot, slot_numbers)
    slot_counts = jnp.take(lon_counts, latitudes)

    def one_slot(inputs):
        matrix, lon_count = inputs
        lon_table = longitude_table(wavenumbers, lon_count, LONS)
        return jnp.dot(matrix, lon_table, preferred_element_type=jnp.float32).astype(jnp.bfloat16)

    gridded = lax.map(one_slot, (rows_by_slot, slot_counts))
    gridded = gridded.reshape(lat_local, 2, 2, lev_local, LONS)
    fields = jnp.transpose(gridded[:, :, 0], (1, 2, 0, 3))
    slopes = jnp.transpose(gridded[:, :, 1], (1, 2, 0, 3))
    return (fields, slopes)


def solution(mesh):
    placed = (
        P(None, None, None, ("set", "lev"), None),
        P(None, "lev", None),
        P(("set", "lev"), None, None),
        P(("set", "lev"), None, None),
        P(("set", "lev")),
        P(),
        P(),
    )
    return jax.shard_map(
        body,
        mesh=mesh,
        in_specs=placed,
        out_specs=(P(None, "lev", "set", None), P(None, "lev", "set", None)),
        check_vma=False,
    )
```

profile of v0, /device:TPU:1, one launch (start us, length us, event | category | flops | bytes accessed | tf_op | source)
XLA Modules:
  0.0 943.5 jit_solution(10823138508034151711)
XLA Ops:
  0.7 0.8 compare_select_fusion.3
  1.4 0.7 compare_and_fusion
  2.1 0.7 broadcast_subtract_fusion.1
  2.8 0.7 fusion.53
  3.6 14.8 %all_gather.6 = bf16[2,128,128]{2,1,0:T(8,128)(2,1)S(1)} all-gather(bf16[2,16,128]{2,1,0:T(8,128)(2,1)} %param.12), channel_id=1, replica_groups=mesh['set'=16,'lev'=8] {'lev'}, dimensions={1}, use_global_device_ids=true | all-gather | bytes 73728 | tf_op jit(solution)/shard_map/all_gather | solution.py:43
  18.4 10.2 %multiply_bitcast_fusion.1 = (bf16[1,2,128,2,5,1281]{2,5,4,3,1,0:T(8,128)(2,1)S(1)}, bf16[1,2,128,2,5,1281]{2,5,4,3,1,0:T(8,128)(2,1)S(1)}) fusion(bf16[5,1281]{1,0:T(8,128)(2,1)S(1)} %get-tuple-element.72, bf16[5,1281]{1,0:T(8,128)(2,1)S(1)} %get-tuple-element.73, bf16[2,128,2,5,1281]{1,2,4,3,0:T(2,128)(2,1)} %param.11, ...), kind=kOutput, calls=%fused_computation.36 | convolution fusion | flops 859192320 | bytes 19792936 | tf_op jit(solution)/shard_map/flk,fkrpj->flrpj/dot_general | solution.py:46
  28.6 6.5 fusion.46
  35.1 6.4 fusion.41
  41.6 1.8 pad_maximum_fusion.1
  43.3 7.6 copy.28
  51.0 5.2 gather_fusion
  56.2 5.7 copy.29
  61.9 21.4 %gather.10 = bf16[2,2,2,8,16,2,5,16,8]{4,3,8,7,6,5,2,1,0:T(8,128)(2,1)} reshape(bf16[2,2,2,128,2,5,128]{3,6,5,4,2,1,0:T(8,128)(2,1)} %copy.29) | data formatting | bytes 5242880 | tf_op jit(solution)/shard_map/jit(_take)/gather | solution.py:58
  83.3 10.9 %select_bitcast_fusion = bf16[16,8,2,2,16,2,8,5,2]{4,1,6,0,7,5,2,8,3:T(8,128)(2,1)S(1)} fusion(bf16[2,2,2,8,16,2,5,16,8]{4,3,8,7,6,5,2,1,0:T(8,128)(2,1)} %gather.10, pred[16,8]{1,0:T(8,128)(4,1)S(1)} %broadcast_in_dim.68), kind=kLoop, calls=%fused_computation.27 | loop fusion | flops 1310720 | bytes 5243008 | tf_op jit(solution)/shard_map/transpose | solution.py:60
  94.3 7.8 copy.30
  102.1 27.9 %reshape.174 = bf16[128,2,5120]{2,1,0:T(2,128)(2,1)} reshape(bf16[128,2,2,2,5,2,8,16]{7,6,5,4,3,2,1,0:T(8,128)(2,1)} %bitcast.78) | data formatting | bytes 5242880
  130.0 9.9 %all-to-all-start = ((bf16[128,2,5120]{2,1,0:T(2,128)(2,1)}), bf16[128,2,5120]{2,1,0:T(2,128)(2,1)}, u32[]{:S(2)}, u32[]{:S(2)}) async-start(bf16[128,2,5120]{2,1,0:T(2,128)(2,1)} %reshape.174), calls=%async_computation | async-start | bytes 5242880 | tf_op jit(solution)/shard_map/all_to_all | solution.py:63
  139.9 0.2 dynamic-update-slice
  140.2 87.0 %all-reduce = s32[640]{0:T(1024)S(1)} all-reduce(s32[640]{0:T(1024)S(1)} %dynamic-update-slice), channel_id=1, replica_groups=mesh['set'=16,'lev'=8] {'set','lev'}, use_global_device_ids=true, to_apply=%add | all-reduce | flops 640 | bytes 5120
  227.2 0.2 copy.32
  227.4 0.2 mul.154
  227.6 0.2 reshape.136
  227.9 0.6 gather_fusion.1
  228.5 0.6 gather_fusion.2
  229.2 22.2 %reshape.175 = bf16[128,2,2,2,5,2,8,16]{7,6,5,4,3,2,1,0:T(8,128)(2,1)} reshape(bf16[128,2,5120]{2,1,0:T(2,128)(2,1)} %all-to-all-done) | data formatting | bytes 5242880
  251.4 11.9 %bitcast_bitcast_fusion = bf16[8,2,2,16,2,128,5,2]{3,0,7,6,4,2,1,5:T(8,128)(2,1)S(1)} fusion(bf16[128,2,2,2,5,2,8,16]{7,6,5,4,3,2,1,0:T(8,128)(2,1)} %reshape.175), kind=kLoop, calls=%fused_computation.67 | loop fusion | bytes 5242880 | tf_op jit(solution)/shard_map/transpose | solution.py:64
  263.3 23.6 %copy.31 = bf16[8,2,2,16,2,128,5,2]{3,2,1,7,6,5,4,0:T(2,128)(2,1)} copy(bf16[8,2,2,16,2,128,5,2]{3,0,7,6,4,2,1,5:T(8,128)(2,1)S(1)} %bitcast_bitcast_fusion) | data formatting | bytes 5242880 | tf_op jit(solution)/shard_map/transpose | solution.py:64
  286.9 36.2 %reshape.135 = bf16[8,64,2560]{1,2,0:T(8,128)(2,1)} reshape(bf16[8,2,2,16,2,128,5,2]{3,2,1,7,6,5,4,0:T(2,128)(2,1)} %copy.31) | data formatting | bytes 5242880 | tf_op jit(solution)/shard_map/reshape | solution.py:65
  323.1 6.1 copy.33
  329.2 612.0 %while.11 = (s32[]{:T(128)}, bf16[8,64,1024]{2,1,0:T(8,128)(2,1)S(1)}, bf16[8,64,2560]{2,1,0:T(8,128)(2,1)}, s32[8]{0:T(128)S(1)}, s32[1280]{0:T(1024)S(1)}, /*i...) while((s32[]{:T(128)}, bf16[8,64,1024]{2,1,0:T(8,128)(2,1)S(1)}, ...), condition=%wide.wide.region_1.3_spmd, body=%wide.wide.region_0.2_spmd.sunk | while | flops 367072000 | bytes 10978481 | solution.py:76
  329.2 0.6 dynamic_slice.17
  331.5 0.6 iota_compare_fusion.4
  332.1 71.5 %select_convert_fusion.4 = (bf16[1280,1024]{1,0:T(8,128)(2,1)S(1)}, bf16[1280,1024]{1,0:T(8,128)(2,1)S(1)}) fusion(f32[]{:T(128)S(6)} %div.15, s32[]{:T(128)S(6)} %select_n.105, s32[1280]{0:T(1024)S(1)} %get-tuple-element.179, f32[1280]{0:T(1024)S(1)} %get-tuple-element.149, pred[]{:T(512)S(6)} %lt.76, ...), kind=kLoop, calls=%fused_computation.11.clone.clone.1 | loop fusion | flops 20971520 | bytes 5259273 | tf_op jit(solution)/shard_map/convert
  403.7 2.0 fusion.69
  405.7 0.6 dynamic_slice.17
  408.0 0.6 iota_compare_fusion.4
  408.6 71.5 %select_convert_fusion.4 = (bf16[1280,1024]{1,0:T(8,128)(2,1)S(1)}, bf16[1280,1024]{1,0:T(8,128)(2,1)S(1)}) fusion(f32[]{:T(128)S(6)} %div.15, s32[]{:T(128)S(6)} %select_n.105, s32[1280]{0:T(1024)S(1)} %get-tuple-element.179, f32[1280]{0:T(1024)S(1)} %get-tuple-element.149, pred[]{:T(512)S(6)} %lt.76, ...), kind=kLoop, calls=%fused_computation.11.clone.clone.1 | loop fusion | flops 20971520 | bytes 5259273 | tf_op jit(solution)/shard_map/convert
  480.2 2.0 fusion.69
  482.2 0.6 dynamic_slice.17
  484.5 0.6 iota_compare_fusion.4
  485.1 71.5 %select_convert_fusion.4 = (bf16[1280,1024]{1,0:T(8,128)(2,1)S(1)}, bf16[1280,1024]{1,0:T(8,128)(2,1)S(1)}) fusion(f32[]{:T(128)S(6)} %div.15, s32[]{:T(128)S(6)} %select_n.105, s32[1280]{0:T(1024)S(1)} %get-tuple-element.179, f32[1280]{0:T(1024)S(1)} %get-tuple-element.149, pred[]{:T(512)S(6)} %lt.76, ...), kind=kLoop, calls=%fused_computation.11.clone.clone.1 | loop fusion | flops 20971520 | bytes 5259273 | tf_op jit(solution)/shard_map/convert
  556.7 2.0 fusion.69
  558.7 0.6 dynamic_slice.17
  561.0 0.6 iota_compare_fusion.4
  561.6 71.5 %select_convert_fusion.4 = (bf16[1280,1024]{1,0:T(8,128)(2,1)S(1)}, bf16[1280,1024]{1,0:T(8,128)(2,1)S(1)}) fusion(f32[]{:T(128)S(6)} %div.15, s32[]{:T(128)S(6)} %select_n.105, s32[1280]{0:T(1024)S(1)} %get-tuple-element.179, f32[1280]{0:T(1024)S(1)} %get-tuple-element.149, pred[]{:T(512)S(6)} %lt.76, ...), kind=kLoop, calls=%fused_computation.11.clone.clone.1 | loop fusion | flops 20971520 | bytes 5259273 | tf_op jit(solution)/shard_map/convert
  633.2 2.0 fusion.69
  635.2 0.6 dynamic_slice.17
  637.5 0.6 iota_compare_fusion.4
  638.1 71.5 %select_convert_fusion.4 = (bf16[1280,1024]{1,0:T(8,128)(2,1)S(1)}, bf16[1280,1024]{1,0:T(8,128)(2,1)S(1)}) fusion(f32[]{:T(128)S(6)} %div.15, s32[]{:T(128)S(6)} %select_n.105, s32[1280]{0:T(1024)S(1)} %get-tuple-element.179, f32[1280]{0:T(1024)S(1)} %get-tuple-element.149, pred[]{:T(512)S(6)} %lt.76, ...), kind=kLoop, calls=%fused_computation.11.clone.clone.1 | loop fusion | flops 20971520 | bytes 5259273 | tf_op jit(solution)/shard_map/convert
  709.7 2.0 fusion.69
  711.7 0.6 dynamic_slice.17
  714.0 0.6 iota_compare_fusion.4
  714.6 71.5 %select_convert_fusion.4 = (bf16[1280,1024]{1,0:T(8,128)(2,1)S(1)}, bf16[1280,1024]{1,0:T(8,128)(2,1)S(1)}) fusion(f32[]{:T(128)S(6)} %div.15, s32[]{:T(128)S(6)} %select_n.105, s32[1280]{0:T(1024)S(1)} %get-tuple-element.179, f32[1280]{0:T(1024)S(1)} %get-tuple-element.149, pred[]{:T(512)S(6)} %lt.76, ...), kind=kLoop, calls=%fused_computation.11.clone.clone.1 | loop fusion | flops 20971520 | bytes 5259273 | tf_op jit(solution)/shard_map/convert
  786.2 2.0 fusion.69
  788.2 0.6 dynamic_slice.17
  790.5 0.6 iota_compare_fusion.4
  791.1 71.5 %select_convert_fusion.4 = (bf16[1280,1024]{1,0:T(8,128)(2,1)S(1)}, bf16[1280,1024]{1,0:T(8,128)(2,1)S(1)}) fusion(f32[]{:T(128)S(6)} %div.15, s32[]{:T(128)S(6)} %select_n.105, s32[1280]{0:T(1024)S(1)} %get-tuple-element.179, f32[1280]{0:T(1024)S(1)} %get-tuple-element.149, pred[]{:T(512)S(6)} %lt.76, ...), kind=kLoop, calls=%fused_computation.11.clone.clone.1 | loop fusion | flops 20971520 | bytes 5259273 | tf_op jit(solution)/shard_map/convert
  862.7 2.0 fusion.69
  864.7 0.6 dynamic_slice.17
  867.0 0.6 iota_compare_fusion.4
  867.6 71.5 %select_convert_fusion.4 = (bf16[1280,1024]{1,0:T(8,128)(2,1)S(1)}, bf16[1280,1024]{1,0:T(8,128)(2,1)S(1)}) fusion(f32[]{:T(128)S(6)} %div.15, s32[]{:T(128)S(6)} %select_n.105, s32[1280]{0:T(1024)S(1)} %get-tuple-element.179, f32[1280]{0:T(1024)S(1)} %get-tuple-element.149, pred[]{:T(512)S(6)} %lt.76, ...), kind=kLoop, calls=%fused_computation.11.clone.clone.1 | loop fusion | flops 20971520 | bytes 5259273 | tf_op jit(solution)/shard_map/convert
  939.2 2.0 fusion.69
  941.3 1.1 copy.35
  942.4 1.1 copy.36
  (39 shorter events, 0.4 us)
Async XLA Ops:
  0.6 28.0 %copy-start = (bf16[5,1281,128]{2,1,0:T(8,128)(2,1)S(1)}, bf16[5,1281,128]{2,1,0:T(8,128)(2,1)}, u32[]{:S(2)}) copy-start(bf16[5,1281,128]{2,1,0:T(8,128)(2,1)} %param.13) | copy-start | bytes 4919044
  28.6 6.5 copy-start.6
  130.0 9.9 %copy-start.5 = (s32[5]{0:T(128)S(1)}, s32[5]{0:T(128)}, u32[]{:S(2)}) copy-start(s32[5]{0:T(128)} %param.15) | copy-start | bytes 64
  130.0 97.8 %copy-start.2 = (s32[128]{0:T(128)S(1)}, s32[128]{0:T(128)}, u32[]{:S(2)}) copy-start(s32[128]{0:T(128)} %param.16) | copy-start | bytes 1540
  130.0 98.5 %copy-start.3 = (s32[128]{0:T(128)S(1)}, s32[128]{0:T(128)}, u32[]{:S(2)}) copy-start(s32[128]{0:T(128)} %param.17) | copy-start | bytes 1540
  130.0 99.2 %all-to-all-start = ((bf16[128,2,5120]{2,1,0:T(2,128)(2,1)}), bf16[128,2,5120]{2,1,0:T(2,128)(2,1)}, u32[]{:S(2)}, u32[]{:S(2)}) async-start(bf16[128,2,5120]{2,1,0:T(2,128)(2,1)} %reshape.174), calls=%async_computation | async-start | bytes 5242880 | tf_op jit(solution)/shard_map/all_to_all | solution.py:63
  227.4 24.0 %copy-start.4 = (s32[640,2]{1,0:T(8,128)}, s32[640,2]{1,0:T(8,128)S(1)}, u32[]{:S(2)}) copy-start(s32[640,2]{1,0:T(8,128)S(1)} %copy.32) | copy-start | bytes 15364
  941.2 2.3 copy-start.1
where the time goes:
time: 947 us; the launch traced here: 943 us
  other arithmetic  593 us (63%)
  local copies, waits for them, and re-layouts  185 us (20%)
  blocking collectives  102 us (11%)
  matrix products  39.1 us (4%)
  loops' own time  14.4 us (2%)
  starting transfers between devices  9.85 us (1%)
    another operation x8, other arithmetic  572 us
    unnamed x1, blocking collectives  87 us
    unnamed x20, local copies, waits for them, and re-layouts  52.6 us
    reshape x1, local copies, waits for them, and re-layouts, body(): rows_by_slot.reshape(lat_local, 4 * lev_local, 2 * (top_degree + 1))  36.2 us
    transpose x2, local copies, waits for them, and re-layouts, body(): rows_by_slot = jnp.transpose(incoming, (5, 1, 2, 3, 4, 0, 6, 7))  35.5 us
    gather x3, local copies, waits for them, and re-layouts, body(): band_all = jnp.take(band_all, lat_slot, axis=6)  32.3 us
  transfers between devices with their start and end apart: 1, of which 0 were waited for; matrix products, arithmetic and copies ran while one was open for 0% of the time, Pallas kernels for 0%

commit v1 on v0

v1 whole, which is shorter than its diff:
```python
import functools

import jax
import jax.numpy as jnp
from jax import lax
from jax.experimental import pallas as pl
from jax.experimental.pallas import tpu as pltpu
from jax.sharding import PartitionSpec as P

TRUNC = 1279
ROWS = 1281
PAIRS = 5
SETS = 16
LEVS = 8
SLOTS = 8
LONS = 1024
PAD = 1408
BLK = 128
HIGH0 = 640
MESH = pl.DeviceIdType.MESH
F32 = jnp.float32
BF16 = jnp.bfloat16


def iota(shape, dim):
    return lax.broadcasted_iota(jnp.int32, shape, dim)


def turn(x, count, inverse):
    r = x - jnp.floor(x * inverse + 0.5) * count
    t = r * inverse * 3.14159265358979
    t2 = t * t
    sn = t * (1.0 + t2 * (-1 / 6 + t2 * (1 / 120 + t2 * (-1 / 5040 + t2 * (1 / 362880 - t2 * (1 / 39916800))))))
    cs = 1.0 + t2 * (-1 / 2 + t2 * (1 / 24 + t2 * (-1 / 720 + t2 * (1 / 40320 - t2 * (1 / 3628800)))))
    return 1.0 - 2.0 * sn * sn, 2.0 * sn * cs


def kernel(
    spec, vert, tabs_v, tabs_s, wave, lat, counts, lat_row,
    out_f, out_s,
    sbuf, tbuf, tpt, place, abuf, adjf, xbuf, rbuf, dbuf, vall, vt,
    wave_me, wave_set, wave_pack, wave_all, wcol, cval, cinv, psi_c, psi_s,
    table, acc, df, outf, outb,
    sem_s, sem_t, sem_v, sem_w1, sem_w2, sem_send1, sem_recv1, sem_send2, sem_recv2, sem_loc, sem_out,
):
    a = lax.axis_index("set")
    b = lax.axis_index("lev")

    def nth_set(i):
        return lax.rem(a + i, SETS)

    def nth_lev(i):
        return lax.rem(b + i, LEVS)

    def load_tables(p):
        return (
            pltpu.make_async_copy(tabs_v.at[p], tbuf.at[0, p], sem_t.at[0, p]),
            pltpu.make_async_copy(tabs_s.at[p], tbuf.at[1, p], sem_t.at[1, p]),
        )

    def load_spec(p):
        return [
            pltpu.make_async_copy(spec.at[f, p], sbuf.at[f, p, pl.ds(0, ROWS)], sem_s.at[f, p]) for f in range(2)
        ]

    for p in range(PAIRS):
        for c in load_tables(p):
            c.start()
    for p in range(PAIRS):
        for c in load_spec(p):
            c.start()
    own_v = pltpu.make_async_copy(vert, vall.at[b], sem_v.at[2])
    own_v.start()

    bar = pltpu.get_barrier_semaphore()

    @pl.loop(1, LEVS)
    def _(i):
        pl.semaphore_signal(bar, inc=1, device_id=(a, nth_lev(i)), device_id_type=MESH)

    @pl.loop(1, SETS)
    def _(i):
        pl.semaphore_signal(bar, inc=1, device_id=(nth_set(i), b), device_id_type=MESH)

    for f in range(2):
        for p in range(PAIRS):
            sbuf[f, p, ROWS:PAD] = jnp.zeros((PAD - ROWS, 2, 128), BF16)

    lane = iota((8, 128), 1)
    row_of_waves = jnp.zeros((8, 128), F32)
    for p in range(PAIRS):
        row_of_waves = jnp.where(lane == p, wave[p].astype(F32), row_of_waves)
    wave_me[...] = row_of_waves

    sub = iota((8, 128), 0)
    cv = jnp.zeros((8, 128), F32)
    for s in range(SLOTS):
        c_s = counts[lat[a * SLOTS + s]].astype(F32)
        cv = jnp.where(sub == s, c_s, cv)
    cval[...] = cv
    cinv[...] = 1.0 / cv
    for t in range(LONS // 128):
        x = ((iota((8, 128), 1) + t * 128) * TRUNC).astype(F32)
        pc, ps = turn(x, cval[...], cinv[...])
        psi_c[:, t * 128 : t * 128 + 128] = pc
        psi_s[:, t * 128 : t * 128 + 128] = ps

    @pl.loop(0, 8)
    def _(i):
        row = iota((128, 1024), 0)
        col = iota((128, 1024), 1)
        h, f, r = i // 4, (i // 2) % 2, i % 2
        want = (row // 16) * 128 + h * 64 + r * 32 + f * 16 + row % 16
        place[pl.ds(pl.multiple_of(i * 128, 128), 128), :] = jnp.where(col == want, 1.0, 0.0).astype(BF16)

    r_row = iota((256, 128), 0)
    pick = jnp.where(iota((256, 128), 1) == (r_row // 16) * 8 + r_row % 8, 1.0, 0.0).astype(BF16)
    lat_b = jnp.broadcast_to(lat_row[...], (128, 128)).astype(F32).astype(BF16)
    lat_col = lax.dot_general(pick, lat_b, (((1,), (1,)), ((), ())), preferred_element_type=F32)
    hit = lat_col == iota((256, 128), 1).astype(F32)
    k_row = (r_row // 8) % 2
    order = jnp.concatenate(
        [
            jnp.where(jnp.logical_and(hit, k_row == 0), 1.0, 0.0),
            jnp.where(jnp.logical_and(hit, k_row == 1), 1.0, 0.0),
        ],
        axis=1,
    ).astype(BF16)

    @pl.loop(0, PAIRS)
    def _(p):
        for c in load_tables(p):
            c.wait()

        @pl.loop(0, 5)
        def _(t):
            j0 = pl.multiple_of(t * 256, 256)
            both = jnp.concatenate([tbuf[0, p, pl.ds(j0, 256)], tbuf[1, p, pl.ds(j0, 256)]], axis=1)
            turned = lax.dot_general(order, both, (((1,), (1,)), ((), ())), preferred_element_type=F32)
            tpt[p, :, pl.ds(j0, 256)] = turned.astype(BF16)

        last = jnp.concatenate([tbuf[0, p, 1280:1281], tbuf[1, p, 1280:1281]], axis=1).astype(F32)
        last = jnp.broadcast_to(last, (128, 256))
        last = jnp.where(iota((128, 256), 0) == 0, last, 0.0).astype(BF16)
        turned = lax.dot_general(order, last, (((1,), (1,)), ((), ())), preferred_element_type=F32)
        tpt[p, :, 1280:PAD] = turned.astype(BF16)

    own_v.wait()
    pl.semaphore_wait(bar, LEVS - 1 + SETS - 1)

    @pl.loop(1, LEVS)
    def _(i):
        pltpu.make_async_remote_copy(
            src_ref=vall.at[b], dst_ref=vall.at[b], send_sem=sem_v.at[0], recv_sem=sem_v.at[1],
            device_id=(a, nth_lev(i)), device_id_type=MESH,
        ).start()

    @pl.loop(1, SETS)
    def _(i):
        pltpu.make_async_remote_copy(
            src_ref=wave_me, dst_ref=wave_set.at[a], send_sem=sem_w1.at[0], recv_sem=sem_w1.at[1],
            device_id=(nth_set(i), b), device_id_type=MESH,
        ).start()

    for e in range(2):
        pltpu.make_async_copy(vall.at[pl.ds(0, LEVS - 1)], vall.at[pl.ds(0, LEVS - 1)], sem_v.at[e]).wait()
    for f in range(2):
        vt[f] = vall[:, f].reshape(128, 128).astype(F32).T.astype(BF16)

    def send1(p):
        pltpu.make_async_copy(xbuf.at[p, a], rbuf.at[p, a], sem_loc.at[0, p]).start()

        @pl.loop(1, SETS)
        def _(i):
            t = nth_set(i)
            pltpu.make_async_remote_copy(
                src_ref=xbuf.at[p, t], dst_ref=rbuf.at[p, a], send_sem=sem_send1.at[p], recv_sem=sem_recv1.at[p],
                device_id=(t, b), device_id_type=MESH,
            ).start()

    def send2(p):
        pltpu.make_async_copy(xbuf.at[p, a], rbuf.at[p, a], sem_loc.at[0, p]).wait()
        pltpu.make_async_copy(
            xbuf.at[p, pl.ds(0, SETS - 1)], rbuf.at[p, pl.ds(0, SETS - 1)], sem_recv1.at[p]
        ).wait()
        pltpu.make_async_copy(rbuf.at[p, :, b], dbuf.at[p, b], sem_loc.at[1, p]).start()

        @pl.loop(1, LEVS)
        def _(i):
            t = nth_lev(i)
            pltpu.make_async_remote_copy(
                src_ref=rbuf.at[p, :, t], dst_ref=dbuf.at[p, b], send_sem=sem_send2.at[p], recv_sem=sem_recv2.at[p],
                device_id=(a, t), device_id_type=MESH,
            ).start()

    def wait2(p):
        pltpu.make_async_copy(rbuf.at[p, :, b], dbuf.at[p, b], sem_loc.at[1, p]).wait()
        pltpu.make_async_copy(
            dbuf.at[p, pl.ds(0, LEVS - 1)], dbuf.at[p, pl.ds(0, LEVS - 1)], sem_recv2.at[p]
        ).wait()

    def waits_of_sends(p):
        pltpu.make_async_copy(
            xbuf.at[p, pl.ds(0, SETS - 1)], rbuf.at[p, pl.ds(0, SETS - 1)], sem_send1.at[p]
        ).wait()
        pltpu.make_async_copy(
            dbuf.at[p, pl.ds(0, LEVS - 1)], dbuf.at[p, pl.ds(0, LEVS - 1)], sem_send2.at[p]
        ).wait()

    def legendre(p):
        m = wave[p]
        for c in load_spec(p):
            c.wait()

        @pl.loop(0, PAD // BLK)
        def _(t):
            j0 = pl.multiple_of(t * BLK, BLK)
            j = iota((2 * BLK, 128), 0) // 2 + j0
            degree = jnp.where(j <= TRUNC - m, m + j, j - 1)
            scale = (degree * (degree + 1)).astype(F32) * (1.0 / (TRUNC * (TRUNC + 1)))
            for f in range(2):
                x = sbuf[f, p, pl.ds(j0, BLK)].reshape(2 * BLK, 128)
                coupled = jnp.dot(x, vt[f], preferred_element_type=F32)
                adjf[f] = x.astype(F32) + scale * coupled
                for r in range(2):
                    abuf[pl.ds(j0, BLK), (2 * f + r) * 128 : (2 * f + r + 1) * 128] = adjf[
                        f, pl.ds(r, BLK, stride=2), :
                    ].astype(BF16)

        w_low = jnp.where(m == 0, 1.0, 2.0)
        jl = iota((256, HIGH0), 1) + HIGH0
        edge = tpt[p, :, HIGH0:1280].astype(F32)
        low_hi = jnp.where(jl <= TRUNC - m, edge * w_low, 0.0).astype(BF16)
        low = jnp.dot(
            (tpt[p, :, 0:HIGH0].astype(F32) * w_low).astype(BF16), abuf[0:HIGH0, :], preferred_element_type=F32
        )
        low = low + jnp.dot(low_hi, abuf[HIGH0:1280, :], preferred_element_type=F32)
        jh = iota((256, PAD - HIGH0), 1) + HIGH0
        keep = jnp.logical_and(jh > TRUNC - m, jh < ROWS)
        high_t = jnp.where(keep, tpt[p, :, HIGH0:PAD].astype(F32) * 2.0, 0.0).astype(BF16)
        high = jnp.dot(high_t, abuf[HIGH0:PAD, :], preferred_element_type=F32)
        band = jnp.concatenate([low.astype(BF16), high.astype(BF16)], axis=1)
        for q in range(4):
            placed = jnp.dot(band, place[:, q * 256 : q * 256 + 256], preferred_element_type=F32).astype(BF16)
            for e in range(2):
                for s in range(SETS):
                    xbuf[p, s, 2 * q + e] = placed[16 * s : 16 * s + 16, 128 * e : 128 * e + 128]

    def pass_waves():
        for e in range(2):
            pltpu.make_async_copy(
                wave_set.at[pl.ds(0, SETS - 1)], wave_set.at[pl.ds(0, SETS - 1)], sem_w1.at[e]
            ).wait()
        wave_set[a] = wave_me[...]
        packed = wave_set[:, 0, :]
        wave_pack[...] = packed
        wave_all[b] = packed

        @pl.loop(1, LEVS)
        def _(i):
            pltpu.make_async_remote_copy(
                src_ref=wave_pack, dst_ref=wave_all.at[b], send_sem=sem_w2.at[0], recv_sem=sem_w2.at[1],
                device_id=(a, nth_lev(i)), device_id_type=MESH,
            ).start()

    @pl.loop(0, PAIRS)
    def _(p):
        legendre(p)
        send1(p)

        @pl.when(p == 0)
        def _():
            pass_waves()

        @pl.when(p >= 2)
        def _():
            send2(p - 2)

    for e in range(2):
        pltpu.make_async_copy(
            wave_all.at[pl.ds(0, LEVS - 1)], wave_all.at[pl.ds(0, LEVS - 1)], sem_w2.at[e]
        ).wait()

    def tables(p):
        waves = wave_all[...].reshape(128, 128)
        mine = jnp.sum(jnp.where(iota((128, 128), 1) == p, waves, 0.0), axis=1, keepdims=True)
        wcol[...] = jnp.broadcast_to(mine, (128, 128))

        @pl.loop(0, SLOTS)
        def _(s):
            count = cval[pl.ds(s, 1), :]
            inverse = cinv[pl.ds(s, 1), :]
            for g in range(4):
                rows = slice(32 * g, 32 * g + 32)
                m = wcol[rows, :]
                c, n = turn(m * iota((32, 128), 1).astype(F32), count, inverse)
                sc, sn = turn(m * 128.0, count, inverse)
                for t in range(LONS // 128):
                    table[p, s, rows, 128 * t : 128 * t + 128] = c.astype(BF16)
                    table[p, s, 128 + 32 * g : 160 + 32 * g, 128 * t : 128 * t + 128] = n.astype(BF16)
                    if t < LONS // 128 - 1:
                        c, n = c * sc - n * sn, n * sc + c * sn

    @pl.loop(0, PAIRS)
    def _(p):
        tables(p)

        @pl.when(p == 0)
        def _():
            send2(3)

        @pl.when(p == 2)
        def _():
            send2(4)

    def sums(p, s):
        cos_rows, sin_rows = [[], [], []], [[], [], []]
        for k in range(2):
            x = df[pl.ds(k * 8 + s, 128, stride=16), :].T
            re0, im0, re1, im1 = x[0:32], x[32:64], x[64:96], x[96:128]
            for g, v in enumerate((re0, re1, -im1)):
                cos_rows[g].append(v)
            for g, v in enumerate((-im0, im1, re1)):
                sin_rows[g].append(v)
        cos_side = jnp.concatenate(cos_rows[0] + cos_rows[1] + cos_rows[2], axis=0)
        sin_side = jnp.concatenate(sin_rows[0] + sin_rows[1] + sin_rows[2], axis=0)
        both = jnp.concatenate([cos_side, sin_side], axis=1).astype(BF16)
        return lambda t: jnp.dot(both, table[p, s, :, 256 * t : 256 * t + 256], preferred_element_type=F32)

    @pl.loop(0, PAIRS)
    def _(p):
        wait2(p)
        df[...] = dbuf[p].reshape(2048, 128).astype(F32)

        @pl.loop(0, SLOTS)
        def _(s):
            part = sums(p, s)

            @pl.when(p == 0)
            def _():
                for t in range(4):
                    acc[s, :, 256 * t : 256 * t + 256] = part(t)

            @pl.when(jnp.logical_and(p > 0, p < PAIRS - 1))
            def _():
                for t in range(4):
                    acc[s, :, 256 * t : 256 * t + 256] += part(t)

            @pl.when(p == PAIRS - 1)
            def _():
                for t in range(4):
                    cols = slice(256 * t, 256 * t + 256)
                    total = acc[s, :, cols] + part(t)
                    pc = psi_c[pl.ds(s, 1), cols]
                    ps = psi_s[pl.ds(s, 1), cols]
                    o = total[0:64] + pc * total[64:128] + ps * total[128:192]
                    lon = (iota((64, 256), 1) + 256 * t).astype(F32)
                    count = jnp.concatenate([cval[pl.ds(s, 1), :]] * 2, axis=1)
                    o = jnp.where(lon < count, o, 0.0)
                    for e in range(2):
                        outf[2 * t + e, pl.ds(s, 64, stride=8), :] = o[:, 128 * e : 128 * e + 128]

    for t in range(8):
        outb[:, :, :, :, 128 * t : 128 * t + 128] = outf[t].reshape(2, 2, 16, 8, 128).astype(BF16)
    done = [
        pltpu.make_async_copy(outb.at[0], out_f, sem_out.at[0]),
        pltpu.make_async_copy(outb.at[1], out_s, sem_out.at[1]),
    ]
    for c in done:
        c.start()

    @pl.loop(0, PAIRS)
    def _(p):
        waits_of_sends(p)

    for c in done:
        c.wait()


def body(spectral, vertical, value_table, slope_table, wave_low, lat_slot, lon_counts):
    rows_first = jnp.transpose(spectral, (0, 3, 4, 2, 1))
    anywhere = pl.BlockSpec(memory_space=pl.ANY)
    scalars = pl.BlockSpec(memory_space=pltpu.SMEM)
    dma = pltpu.SemaphoreType.DMA
    out = jax.ShapeDtypeStruct((2, 16, SLOTS, LONS), BF16)
    return pl.pallas_call(
        kernel,
        out_shape=(out, out),
        in_specs=[anywhere] * 4 + [scalars] * 3 + [pl.BlockSpec(memory_space=pltpu.VMEM)],
        out_specs=(anywhere, anywhere),
        scratch_shapes=[
            pltpu.VMEM((2, PAIRS, PAD, 2, 128), BF16),
            pltpu.VMEM((2, PAIRS, ROWS, 128), BF16),
            pltpu.VMEM((PAIRS, 256, PAD), BF16),
            pltpu.VMEM((1024, 1024), BF16),
            pltpu.VMEM((PAD, 512), BF16),
            pltpu.VMEM((2, 2 * BLK, 128), F32),
            pltpu.VMEM((PAIRS, SETS, LEVS, 16, 128), BF16),
            pltpu.VMEM((PAIRS, SETS, LEVS, 16, 128), BF16),
            pltpu.VMEM((PAIRS, LEVS, SETS, 16, 128), BF16),
            pltpu.VMEM((LEVS, 2, 16, 128), BF16),
            pltpu.VMEM((2, 128, 128), BF16),
            pltpu.VMEM((8, 128), F32),
            pltpu.VMEM((SETS, 8, 128), F32),
            pltpu.VMEM((SETS, 128), F32),
            pltpu.VMEM((LEVS, SETS, 128), F32),
            pltpu.VMEM((128, 128), F32),
            pltpu.VMEM((8, 128), F32),
            pltpu.VMEM((8, 128), F32),
            pltpu.VMEM((8, LONS), F32),
            pltpu.VMEM((8, LONS), F32),
            pltpu.VMEM((PAIRS, SLOTS, 256, LONS), BF16),
            pltpu.VMEM((SLOTS, 192, LONS), F32),
            pltpu.VMEM((2048, 128), F32),
            pltpu.VMEM((8, 512, 128), F32),
            pltpu.VMEM((2, 2, 16, SLOTS, LONS), BF16),
            dma((2, PAIRS)),
            dma((2, PAIRS)),
            dma((3,)),
            dma((2,)),
            dma((2,)),
            dma((PAIRS,)),
            dma((PAIRS,)),
            dma((PAIRS,)),
            dma((PAIRS,)),
            dma((2, PAIRS)),
            dma((2,)),
        ],
        compiler_params=pltpu.CompilerParams(
            collective_id=0, has_side_effects=True, vmem_limit_bytes=62 * 2**20
        ),
    )(
        rows_first, vertical, value_table, slope_table, wave_low, lat_slot, lon_counts,
        lat_slot.reshape(1, 128),
    )


def solution(mesh):
    placed = (
        P(None, None, None, ("set", "lev"), None),
        P(None, "lev", None),
        P(("set", "lev"), None, None),
        P(("set", "lev"), None, None),
        P(("set", "lev")),
        P(),
        P(),
    )
    return jax.shard_map(
        body,
        mesh=mesh,
        in_specs=placed,
        out_specs=(P(None, "lev", "set", None), P(None, "lev", "set", None)),
        check_vma=False,
    )
```

time: 947 us -> 84.6 us (0.09)
  the two profiles are of different devices: /device:TPU:1 before, /device:TPU:6 now
where the time goes in v1:
time: 84.6 us; the launch traced here: 84.4 us
  Pallas kernels  80 us (95%)
  local copies, waits for them, and re-layouts  3.74 us (4%)
    pallas_call x1, Pallas kernels, body(): pl.pallas_call(kernel, out_shape=(out, out), in_specs=[anywhere] * 4 + [s...  80 us
    unnamed x2, local copies, waits for them, and re-layouts  3.74 us

profile of v1, /device:TPU:6, one launch (start us, length us, event | category | flops | bytes accessed | tf_op | source)
XLA Modules:
  0.0 84.4 jit_solution(8564347191754485164)
XLA Ops:
  0.6 80.0 %shard_map.86 = (bf16[2,16,8,1024]{3,2,1,0:T(8,128)(2,1)}, bf16[2,16,8,1024]{3,2,1,0:T(8,128)(2,1)}) custom-call(bf16[2,5,1281,2,128]{4,3,2,1,0:T(2,128)(2,1)} %bitcast.2, bf16[2,16,128]{2,1,0:T(8,128)(2,1)} %vert.1, bf16[5,1281,128]{2,1,0:T(8,128)(2,1)} %tabs_v.1, bf16[5,1281,128]{2,1,0:T(8,128)(2,1)} %tabs_s.1, s32[5]{0:T(128)} %wave.1, s32[128]{0:T(128)} %lat.1, ...), custom_call_target="tpu_custom_call" | custom-call | tf_op jit(solution)/shard_map/pallas_call | solution.py:386
  80.6 1.9 %copy.11 = bf16[2,16,8,1024]{3,2,1,0:T(8,128)(2,1)} copy(bf16[2,16,8,1024]{3,2,1,0:T(8,128)(2,1)} %get-tuple-element.4) | data formatting | bytes 1048576
  82.5 1.9 %copy.12 = bf16[2,16,8,1024]{3,2,1,0:T(8,128)(2,1)} copy(bf16[2,16,8,1024]{3,2,1,0:T(8,128)(2,1)} %get-tuple-element.5) | data formatting | bytes 1048576

commit v2 on v1

--- a/solution.py
+++ b/solution.py
@@ -14,8 +14,9 @@
 LEVS = 8
 SLOTS = 8
 LONS = 1024
+SPAN = 512
 PAD = 1408
-BLK = 128
+BLK = 352
 HIGH0 = 640
 MESH = pl.DeviceIdType.MESH
 F32 = jnp.float32
@@ -27,24 +28,25 @@
 
 
 def turn(x, count, inverse):
-    r = x - jnp.floor(x * inverse + 0.5) * count
-    t = r * inverse * 3.14159265358979
+    t = x * inverse
+    t = (x - jnp.floor(t + 0.5) * count) * inverse
     t2 = t * t
-    sn = t * (1.0 + t2 * (-1 / 6 + t2 * (1 / 120 + t2 * (-1 / 5040 + t2 * (1 / 362880 - t2 * (1 / 39916800))))))
-    cs = 1.0 + t2 * (-1 / 2 + t2 * (1 / 24 + t2 * (-1 / 720 + t2 * (1 / 40320 - t2 * (1 / 3628800)))))
+    sn = t * (3.141590284 + t2 * (-5.167407698 + t2 * (2.544020811 + t2 * (-0.559489909))))
+    cs = 0.999993295 + t2 * (-4.933938015 + t2 * (4.041283824 + t2 * (-1.222127058)))
     return 1.0 - 2.0 * sn * sn, 2.0 * sn * cs
 
 
 def kernel(
     spec, vert, tabs_v, tabs_s, wave, lat, counts, lat_row,
     out_f, out_s,
-    sbuf, tbuf, tpt, place, abuf, adjf, xbuf, rbuf, dbuf, vall, vt,
-    wave_me, wave_set, wave_pack, wave_all, wcol, cval, cinv, psi_c, psi_s,
-    table, acc, df, outf, outb,
-    sem_s, sem_t, sem_v, sem_w1, sem_w2, sem_send1, sem_recv1, sem_send2, sem_recv2, sem_loc, sem_out,
+    sbuf, slast, tbuf, tpt, place, abuf, adjf, xbuf, ra, rb, dbuf, vall, vt,
+    wave_me, wave_set, wave_pack, wave_all, wcol, wave_t, shift, step, clane, cval, cinv, psi_c, psi_s,
+    table, lhs, acc, df, outf, outb,
+    sem_s, sem_t, sem_v, sem_w1, sem_w2, sem_a1, sem_b1, sem_a2, sem_b2, sem_loc, sem_out,
 ):
     a = lax.axis_index("set")
     b = lax.axis_index("lev")
+    y, core = b // 2, lax.rem(b, 2)
 
     def nth_set(i):
         return lax.rem(a + i, SETS)
@@ -59,9 +61,16 @@
         )
 
     def load_spec(p):
-        return [
-            pltpu.make_async_copy(spec.at[f, p], sbuf.at[f, p, pl.ds(0, ROWS)], sem_s.at[f, p]) for f in range(2)
+        whole = [
+            pltpu.make_async_copy(
+                spec.at[f, p, pl.ds(0, 1280)].reshape(2560, 128), sbuf.at[f, p, pl.ds(0, 2560)], sem_s.at[f, p]
+            )
+            for f in range(2)
         ]
+        tail = [
+            pltpu.make_async_copy(spec.at[f, p, pl.ds(1280, 1)], slast.at[f, p], sem_s.at[2 + f, p]) for f in range(2)
+        ]
+        return whole + tail
 
     for p in range(PAIRS):
         for c in load_tables(p):
@@ -84,7 +93,7 @@
 
     for f in range(2):
         for p in range(PAIRS):
-            sbuf[f, p, ROWS:PAD] = jnp.zeros((PAD - ROWS, 2, 128), BF16)
+            sbuf[f, p, 2576 : 2 * PAD] = jnp.zeros((2 * PAD - 2576, 128), BF16)
 
     lane = iota((8, 128), 1)
     row_of_waves = jnp.zeros((8, 128), F32)
@@ -98,6 +107,12 @@
         c_s = counts[lat[a * SLOTS + s]].astype(F32)
         cv = jnp.where(sub == s, c_s, cv)
     cval[...] = cv
+    clane_row = jnp.ones((1, 128), F32)
+    for s in range(SLOTS):
+        c_s = counts[lat[a * SLOTS + s]].astype(F32)
+        clane_row = jnp.where(iota((1, 128), 1) == s, c_s, clane_row)
+    clane[0:1, :] = clane_row
+    clane[1:2, :] = 1.0 / clane_row
     cinv[...] = 1.0 / cv
     for t in range(LONS // 128):
         x = ((iota((8, 128), 1) + t * 128) * TRUNC).astype(F32)
@@ -167,50 +182,109 @@
     for f in range(2):
         vt[f] = vall[:, f].reshape(128, 128).astype(F32).T.astype(BF16)
 
+    def local(p, n):
+        src, dst = (
+            (xbuf.at[p, a, 0], ra.at[p, a]),
+            (ra.at[p, :, y], dbuf.at[p, b]),
+            (xbuf.at[p, :, 1, y], rb.at[p, b]),
+            (rb.at[p, :, a], dbuf.at[p, :, a]),
+        )[n]
+        return pltpu.make_async_copy(src, dst, sem_loc.at[n, p])
+
+    def wait_bytes(ref, sem):
+        pltpu.make_async_copy(ref, ref, sem).wait()
+
+    def to_lev(p, core_to, src, dst, sems):
+        def one(i):
+            t = lax.rem(y + i, 4)
+            pltpu.make_async_remote_copy(
+                src_ref=src(t), dst_ref=dst, send_sem=sems.at[0, p], recv_sem=sems.at[1, p],
+                device_id=(a, 2 * t + core_to), device_id_type=MESH,
+            ).start()
+
+        @pl.loop(1, 4)
+        def _(i):
+            one(i)
+
+        @pl.when(core != core_to)
+        def _():
+            one(0)
+
+    def wait_sent_lev(p, core_to, sems):
+        wait_bytes(dbuf.at[p, pl.ds(0, 3)], sems.at[0, p])
+
+        @pl.when(core != core_to)
+        def _():
+            wait_bytes(dbuf.at[p, 0], sems.at[0, p])
+
     def send1(p):
-        pltpu.make_async_copy(xbuf.at[p, a], rbuf.at[p, a], sem_loc.at[0, p]).start()
+        local(p, 0).start()
 
         @pl.loop(1, SETS)
         def _(i):
             t = nth_set(i)
             pltpu.make_async_remote_copy(
-                src_ref=xbuf.at[p, t], dst_ref=rbuf.at[p, a], send_sem=sem_send1.at[p], recv_sem=sem_recv1.at[p],
+                src_ref=xbuf.at[p, t, 0], dst_ref=ra.at[p, a], send_sem=sem_a1.at[0, p], recv_sem=sem_a1.at[1, p],
                 device_id=(t, b), device_id_type=MESH,
             ).start()
 
+        to_lev(p, 1, lambda t: xbuf.at[p, :, 1, t], rb.at[p, b], sem_b1)
+
+        @pl.when(core == 1)
+        def _():
+            local(p, 2).start()
+
     def send2(p):
-        pltpu.make_async_copy(xbuf.at[p, a], rbuf.at[p, a], sem_loc.at[0, p]).wait()
-        pltpu.make_async_copy(
-            xbuf.at[p, pl.ds(0, SETS - 1)], rbuf.at[p, pl.ds(0, SETS - 1)], sem_recv1.at[p]
-        ).wait()
-        pltpu.make_async_copy(rbuf.at[p, :, b], dbuf.at[p, b], sem_loc.at[1, p]).start()
-
-        @pl.loop(1, LEVS)
-        def _(i):
-            t = nth_lev(i)
-            pltpu.make_async_remote_copy(
-                src_ref=rbuf.at[p, :, t], dst_ref=dbuf.at[p, b], send_sem=sem_send2.at[p], recv_sem=sem_recv2.at[p],
-                device_id=(a, t), device_id_type=MESH,
-            ).start()
+        local(p, 0).wait()
+        wait_bytes(ra.at[p, pl.ds(0, SETS - 1)], sem_a1.at[1, p])
+
+        @pl.when(core == 0)
+        def _():
+            local(p, 1).start()
+
+        to_lev(p, 0, lambda t: ra.at[p, :, t], dbuf.at[p, b], sem_a2)
+
+        @pl.when(core == 1)
+        def _():
+            local(p, 2).wait()
+            wait_bytes(rb.at[p, pl.ds(0, LEVS - 1)], sem_b1.at[1, p])
+            local(p, 3).start()
+
+            @pl.loop(1, SETS)
+            def _(i):
+                t = nth_set(i)
+                pltpu.make_async_remote_copy(
+                    src_ref=rb.at[p, :, t], dst_ref=dbuf.at[p, :, a],
+                    send_sem=sem_b2.at[0, p], recv_sem=sem_b2.at[1, p], device_id=(t, b), device_id_type=MESH,
+                ).start()
 
     def wait2(p):
-        pltpu.make_async_copy(rbuf.at[p, :, b], dbuf.at[p, b], sem_loc.at[1, p]).wait()
-        pltpu.make_async_copy(
-            dbuf.at[p, pl.ds(0, LEVS - 1)], dbuf.at[p, pl.ds(0, LEVS - 1)], sem_recv2.at[p]
-        ).wait()
+        @pl.when(core == 0)
+        def _():
+            local(p, 1).wait()
+            wait_bytes(dbuf.at[p, pl.ds(0, LEVS - 1)], sem_a2.at[1, p])
+
+        @pl.when(core == 1)
+        def _():
+            local(p, 3).wait()
+            wait_bytes(dbuf.at[p, :, pl.ds(0, SETS - 1)], sem_b2.at[1, p])
 
     def waits_of_sends(p):
-        pltpu.make_async_copy(
-            xbuf.at[p, pl.ds(0, SETS - 1)], rbuf.at[p, pl.ds(0, SETS - 1)], sem_send1.at[p]
-        ).wait()
-        pltpu.make_async_copy(
-            dbuf.at[p, pl.ds(0, LEVS - 1)], dbuf.at[p, pl.ds(0, LEVS - 1)], sem_send2.at[p]
-        ).wait()
+        wait_bytes(ra.at[p, pl.ds(0, SETS - 1)], sem_a1.at[0, p])
+        wait_sent_lev(p, 1, sem_b1)
+        wait_sent_lev(p, 0, sem_a2)
+
+        @pl.when(core == 1)
+        def _():
+            wait_bytes(dbuf.at[p, :, pl.ds(0, SETS - 1)], sem_b2.at[0, p])
 
     def legendre(p):
         m = wave[p]
         for c in load_spec(p):
             c.wait()
+        for f in range(2):
+            end = slast[f, p].reshape(2, 128).astype(F32)
+            sbuf[f, p, 2560:2576] = jnp.concatenate([end, jnp.zeros((14, 128), F32)], axis=0).astype(BF16)
 
         @pl.loop(0, PAD // BLK)
         def _(t):
@@ -219,7 +293,7 @@
             degree = jnp.where(j <= TRUNC - m, m + j, j - 1)
             scale = (degree * (degree + 1)).astype(F32) * (1.0 / (TRUNC * (TRUNC + 1)))
             for f in range(2):
-                x = sbuf[f, p, pl.ds(j0, BLK)].reshape(2 * BLK, 128)
+                x = sbuf[f, p, pl.ds(pl.multiple_of(2 * t * BLK, 2 * BLK), 2 * BLK), :]
                 coupled = jnp.dot(x, vt[f], preferred_element_type=F32)
                 adjf[f] = x.astype(F32) + scale * coupled
                 for r in range(2):
@@ -244,7 +318,7 @@
             placed = jnp.dot(band, place[:, q * 256 : q * 256 + 256], preferred_element_type=F32).astype(BF16)
             for e in range(2):
                 for s in range(SETS):
-                    xbuf[p, s, 2 * q + e] = placed[16 * s : 16 * s + 16, 128 * e : 128 * e + 128]
+                    xbuf[p, s, e, q] = placed[16 * s : 16 * s + 16, 128 * e : 128 * e + 128]
 
     def pass_waves():
         for e in range(2):
@@ -281,84 +355,106 @@
             wave_all.at[pl.ds(0, LEVS - 1)], wave_all.at[pl.ds(0, LEVS - 1)], sem_w2.at[e]
         ).wait()
 
+    wave_t[...] = wave_all[...].reshape(128, 128).T
+
     def tables(p):
         waves = wave_all[...].reshape(128, 128)
         mine = jnp.sum(jnp.where(iota((128, 128), 1) == p, waves, 0.0), axis=1, keepdims=True)
-        wcol[...] = jnp.broadcast_to(mine, (128, 128))
+        m_all = jnp.broadcast_to(mine, (128, 128))
+        wcol[...] = m_all
+        sc, sn = turn(m_all * 128.0, clane[0:1, :], clane[1:2, :])
+        m_row = jnp.broadcast_to(wave_t[pl.ds(p, 1), :], (8, 128))
+        shift_c, shift_s = turn(m_row * SPAN, cval[...], cinv[...])
+        shift[p, 0] = shift_c
+        shift[p, 1] = shift_s
+        step[0] = sc
+        step[1] = sn
 
         @pl.loop(0, SLOTS)
         def _(s):
             count = cval[pl.ds(s, 1), :]
             inverse = cinv[pl.ds(s, 1), :]
+            row = pl.multiple_of(p * 256, 256)
+            pick_s = iota((32, 128), 1) == s
             for g in range(4):
                 rows = slice(32 * g, 32 * g + 32)
-                m = wcol[rows, :]
-                c, n = turn(m * iota((32, 128), 1).astype(F32), count, inverse)
-                sc, sn = turn(m * 128.0, count, inverse)
-                for t in range(LONS // 128):
-                    table[p, s, rows, 128 * t : 128 * t + 128] = c.astype(BF16)
-                    table[p, s, 128 + 32 * g : 160 + 32 * g, 128 * t : 128 * t + 128] = n.astype(BF16)
-                    if t < LONS // 128 - 1:
+                c, n = turn(wcol[rows, :] * iota((32, 128), 1).astype(F32), count, inverse)
+                sc, sn = (
+                    jnp.broadcast_to(
+                        jnp.sum(jnp.where(pick_s, step[e, rows, :], 0.0), axis=1, keepdims=True), (32, 128)
+                    )
+                    for e in range(2)
+                )
+                for t in range(SPAN // 128):
+                    table[s, pl.ds(row + 32 * g, 32), 128 * t : 128 * t + 128] = c.astype(BF16)
+                    table[s, pl.ds(row + 128 + 32 * g, 32), 128 * t : 128 * t + 128] = n.astype(BF16)
+                    if t < SPAN // 128 - 1:
                         c, n = c * sc - n * sn, n * sc + c * sn
+
+    def gather(p):
+        wait2(p)
+        df[...] = dbuf[p].reshape(2048, 128).astype(F32)
+
+        @pl.loop(0, SLOTS)
+        def _(s):
+            tc = shift[p, 0, pl.ds(s, 1), :]
+            ts = shift[p, 1, pl.ds(s, 1), :]
+            c0 = pl.multiple_of(p * 256, 256)
+            c1 = pl.multiple_of(c0 + 128, 128)
+            for k in range(2):
+                x = df[pl.ds(k * 8 + s, 128, stride=16), :].T
+                re0, im0, re1, im1 = x[0:32], x[32:64], x[64:96], x[96:128]
+                for t in range(2):
+                    if t == 1:
+                        re0, im0 = re0 * tc - im0 * ts, re0 * ts + im0 * tc
+                        re1, im1 = re1 * tc + im1 * ts, im1 * tc - re1 * ts
+                    for g, (v, w) in enumerate(((re0, -im0), (re1, im1), (-im1, re1))):
+                        row = 192 * t + 64 * g + 32 * k
+                        lhs[s, row : row + 32, pl.ds(c0, 128)] = v.astype(BF16)
+                        lhs[s, row : row + 32, pl.ds(c1, 128)] = w.astype(BF16)
+
+    FIRST = 256 * (PAIRS - 1)
 
     @pl.loop(0, PAIRS)
     def _(p):
         tables(p)
 
-        @pl.when(p == 0)
-        def _():
-            send2(3)
-
-        @pl.when(p == 2)
-        def _():
-            send2(4)
-
-    def sums(p, s):
-        cos_rows, sin_rows = [[], [], []], [[], [], []]
-        for k in range(2):
-            x = df[pl.ds(k * 8 + s, 128, stride=16), :].T
-            re0, im0, re1, im1 = x[0:32], x[32:64], x[64:96], x[96:128]
-            for g, v in enumerate((re0, re1, -im1)):
-                cos_rows[g].append(v)
-            for g, v in enumerate((-im0, im1, re1)):
-                sin_rows[g].append(v)
-        cos_side = jnp.concatenate(cos_rows[0] + cos_rows[1] + cos_rows[2], axis=0)
-        sin_side = jnp.concatenate(sin_rows[0] + sin_rows[1] + sin_rows[2], axis=0)
-        both = jnp.concatenate([cos_side, sin_side], axis=1).astype(BF16)
-        return lambda t: jnp.dot(both, table[p, s, :, 256 * t : 256 * t + 256], preferred_element_type=F32)
-
-    @pl.loop(0, PAIRS)
-    def _(p):
-        wait2(p)
-        df[...] = dbuf[p].reshape(2048, 128).astype(F32)
-
-        @pl.loop(0, SLOTS)
-        def _(s):
-            part = sums(p, s)
-
-            @pl.when(p == 0)
-            def _():
-                for t in range(4):
-                    acc[s, :, 256 * t : 256 * t + 256] = part(t)
-
-            @pl.when(jnp.logical_and(p > 0, p < PAIRS - 1))
-            def _():
-                for t in range(4):
-                    acc[s, :, 256 * t : 256 * t + 256] += part(t)
-
-            @pl.when(p == PAIRS - 1)
-            def _():
-                for t in range(4):
-                    cols = slice(256 * t, 256 * t + 256)
-                    total = acc[s, :, cols] + part(t)
-                    pc = psi_c[pl.ds(s, 1), cols]
-                    ps = psi_s[pl.ds(s, 1), cols]
-                    o = total[0:64] + pc * total[64:128] + ps * total[128:192]
-                    lon = (iota((64, 256), 1) + 256 * t).astype(F32)
-                    count = jnp.concatenate([cval[pl.ds(s, 1), :]] * 2, axis=1)
-                    o = jnp.where(lon < count, o, 0.0)
-                    for e in range(2):
-                        outf[2 * t + e, pl.ds(s, 64, stride=8), :] = o[:, 128 * e : 128 * e + 128]
+        @pl.when(p < 2)
+        def _():
+            send2(p + 3)
+
+        @pl.when(p >= 2)
+        def _():
+            gather(p - 2)
+
+    gather(3)
+
+    @pl.loop(0, SLOTS)
+    def _(s):
+        for t in range(SPAN // 256):
+            cols = slice(256 * t, 256 * t + 256)
+            acc[s, :, cols] = jnp.dot(lhs[s, :, 0:FIRST], table[s, 0:FIRST, cols], preferred_element_type=F32)
+
+    gather(4)
+
+    @pl.loop(0, SLOTS)
+    def _(s):
+        count = jnp.concatenate([cval[pl.ds(s, 1), :]] * 2, axis=1)
+        for t in range(SPAN // 256):
+            cols = slice(256 * t, 256 * t + 256)
+            total = acc[s, :, cols] + jnp.dot(
+                lhs[s, :, FIRST : 256 * PAIRS], table[s, FIRST : 256 * PAIRS, cols], preferred_element_type=F32
+            )
+            for u in range(2):
+                first = SPAN * u + 256 * t
+                pc = psi_c[pl.ds(s, 1), first : first + 256]
+                ps = psi_s[pl.ds(s, 1), first : first + 256]
+                r = 192 * u
+                o = total[r : r + 64] + pc * total[r + 64 : r + 128] + ps * total[r + 128 : r + 192]
+                lon = (iota((64, 256), 1) + first).astype(F32)
+                o = jnp.where(lon < count, o, 0.0)
+                for e in range(2):
+                    outf[first // 128 + e, pl.ds(s, 64, stride=8), :] = o[:, 128 * e : 128 * e + 128]
 
     for t in range(8):
         outb[:, :, :, :, 128 * t : 128 * t + 128] = outf[t].reshape(2, 2, 16, 8, 128).astype(BF16)
@@ -389,14 +485,16 @@
         in_specs=[anywhere] * 4 + [scalars] * 3 + [pl.BlockSpec(memory_space=pltpu.VMEM)],
         out_specs=(anywhere, anywhere),
         scratch_shapes=[
-            pltpu.VMEM((2, PAIRS, PAD, 2, 128), BF16),
+            pltpu.VMEM((2, PAIRS, 2 * PAD, 128), BF16),
+            pltpu.VMEM((2, PAIRS, 1, 2, 128), BF16),
             pltpu.VMEM((2, PAIRS, ROWS, 128), BF16),
             pltpu.VMEM((PAIRS, 256, PAD), BF16),
             pltpu.VMEM((1024, 1024), BF16),
             pltpu.VMEM((PAD, 512), BF16),
             pltpu.VMEM((2, 2 * BLK, 128), F32),
-            pltpu.VMEM((PAIRS, SETS, LEVS, 16, 128), BF16),
-            pltpu.VMEM((PAIRS, SETS, LEVS, 16, 128), BF16),
+            pltpu.VMEM((PAIRS, SETS, 2, 4, 16, 128), BF16),
+            pltpu.VMEM((PAIRS, SETS, 4, 16, 128), BF16),
+            pltpu.VMEM((PAIRS, LEVS, SETS, 16, 128), BF16),
             pltpu.VMEM((PAIRS, LEVS, SETS, 16, 128), BF16),
             pltpu.VMEM((LEVS, 2, 16, 128), BF16),
             pltpu.VMEM((2, 128, 128), BF16),
@@ -405,25 +503,30 @@
             pltpu.VMEM((SETS, 128), F32),
             pltpu.VMEM((LEVS, SETS, 128), F32),
             pltpu.VMEM((128, 128), F32),
+            pltpu.VMEM((128, 128), F32),
+            pltpu.VMEM((PAIRS, 2, 8, 128), F32),
+            pltpu.VMEM((2, 128, 128), F32),
+            pltpu.VMEM((8, 128), F32),
             pltpu.VMEM((8, 128), F32),
             pltpu.VMEM((8, 128), F32),
             pltpu.VMEM((8, LONS), F32),
             pltpu.VMEM((8, LONS), F32),
-            pltpu.VMEM((PAIRS, SLOTS, 256, LONS), BF16),
-            pltpu.VMEM((SLOTS, 192, LONS), F32),
+            pltpu.VMEM((SLOTS, PAIRS * 256, SPAN), BF16),
+            pltpu.VMEM((SLOTS, 384, PAIRS * 256), BF16),
+            pltpu.VMEM((SLOTS, 384, SPAN), F32),
             pltpu.VMEM((2048, 128), F32),
             pltpu.VMEM((8, 512, 128), F32),
             pltpu.VMEM((2, 2, 16, SLOTS, LONS), BF16),
-            dma((2, PAIRS)),
+            dma((4, PAIRS)),
             dma((2, PAIRS)),
             dma((3,)),
             dma((2,)),
             dma((2,)),
-            dma((PAIRS,)),
-            dma((PAIRS,)),
-            dma((PAIRS,)),
-            dma((PAIRS,)),
             dma((2, PAIRS)),
+            dma((2, PAIRS)),
+            dma((2, PAIRS)),
+            dma((2, PAIRS)),
+            dma((4, PAIRS)),
             dma((2,)),
         ],
         compiler_params=pltpu.CompilerParams(

time: 84.6 us -> 69.1 us (0.82)
  the two profiles are of different devices: /device:TPU:6 before, /device:TPU:1 now
where the time goes in v2:
time: 69.1 us; the launch traced here: 68.9 us
  Pallas kernels  64.5 us (93%)
  local copies, waits for them, and re-layouts  3.74 us (5%)
    pallas_call x1, Pallas kernels, body(): pl.pallas_call(kernel, out_shape=(out, out), in_specs=[anywhere] * 4 + [s...  64.5 us
    unnamed x2, local copies, waits for them, and re-layouts  3.74 us

profile of v2, /device:TPU:1, one launch (start us, length us, event | category | flops | bytes accessed | tf_op | source)
XLA Modules:
  0.0 68.9 jit_solution(15343579343520310514)
XLA Ops:
  0.6 64.5 %shard_map.86 = (bf16[2,16,8,1024]{3,2,1,0:T(8,128)(2,1)}, bf16[2,16,8,1024]{3,2,1,0:T(8,128)(2,1)}) custom-call(bf16[2,5,1281,2,128]{4,3,2,1,0:T(2,128)(2,1)} %bitcast.2, bf16[2,16,128]{2,1,0:T(8,128)(2,1)} %vert.1, bf16[5,1281,128]{2,1,0:T(8,128)(2,1)} %tabs_v.1, bf16[5,1281,128]{2,1,0:T(8,128)(2,1)} %tabs_s.1, s32[5]{0:T(128)} %wave.1, s32[128]{0:T(128)} %lat.1, ...), custom_call_target="tpu_custom_call" | custom-call | tf_op jit(solution)/shard_map/pallas_call | solution.py:482
  65.1 1.9 %copy.11 = bf16[2,16,8,1024]{3,2,1,0:T(8,128)(2,1)} copy(bf16[2,16,8,1024]{3,2,1,0:T(8,128)(2,1)} %get-tuple-element.4) | data formatting | bytes 1048576
  67.0 1.9 %copy.12 = bf16[2,16,8,1024]{3,2,1,0:T(8,128)(2,1)} copy(bf16[2,16,8,1024]{3,2,1,0:T(8,128)(2,1)} %get-tuple-element.5) | data formatting | bytes 1048576

commit v3 on v2

--- a/solution.py
+++ b/solution.py
@@ -14,9 +14,9 @@
 LEVS = 8
 SLOTS = 8
 LONS = 1024
-SPAN = 512
+SPAN = 256
 PAD = 1408
-BLK = 352
+BLK = 704
 HIGH0 = 640
 MESH = pl.DeviceIdType.MESH
 F32 = jnp.float32
@@ -55,29 +55,17 @@
         return lax.rem(b + i, LEVS)
 
     def load_tables(p):
-        return (
-            pltpu.make_async_copy(tabs_v.at[p], tbuf.at[0, p], sem_t.at[0, p]),
-            pltpu.make_async_copy(tabs_s.at[p], tbuf.at[1, p], sem_t.at[1, p]),
-        )
+        return [pltpu.make_async_copy(t.at[p], tbuf.at[e, p], sem_t.at[e, p]) for e, t in enumerate((tabs_v, tabs_s))]
 
     def load_spec(p):
-        whole = [
+        return [
             pltpu.make_async_copy(
                 spec.at[f, p, pl.ds(0, 1280)].reshape(2560, 128), sbuf.at[f, p, pl.ds(0, 2560)], sem_s.at[f, p]
             )
             for f in range(2)
         ]
-        tail = [
-            pltpu.make_async_copy(spec.at[f, p, pl.ds(1280, 1)], slast.at[f, p], sem_s.at[2 + f, p]) for f in range(2)
-        ]
-        return whole + tail
-
-    for p in range(PAIRS):
-        for c in load_tables(p):
-            c.start()
-    for p in range(PAIRS):
-        for c in load_spec(p):
-            c.start()
+
+    load_ends = pltpu.make_async_copy(spec.at[:, :, pl.ds(1280, 1)], slast, sem_s.at[2, 0])
     own_v = pltpu.make_async_copy(vert, vall.at[b], sem_v.at[2])
     own_v.start()
 
@@ -91,15 +79,38 @@
     def _(i):
         pl.semaphore_signal(bar, inc=1, device_id=(nth_set(i), b), device_id_type=MESH)
 
-    for f in range(2):
-        for p in range(PAIRS):
-            sbuf[f, p, 2576 : 2 * PAD] = jnp.zeros((2 * PAD - 2576, 128), BF16)
+    def load(p):
+        for c in load_tables(p) + load_spec(p):
+            c.start()
+
+    load(0)
+    load_ends.start()
 
     lane = iota((8, 128), 1)
     row_of_waves = jnp.zeros((8, 128), F32)
     for p in range(PAIRS):
         row_of_waves = jnp.where(lane == p, wave[p].astype(F32), row_of_waves)
     wave_me[...] = row_of_waves
+
+    own_v.wait()
+    pl.semaphore_wait(bar, LEVS - 1 + SETS - 1)
+
+    @pl.loop(1, LEVS)
+    def _(i):
+        pltpu.make_async_remote_copy(
+            src_ref=vall.at[b], dst_ref=vall.at[b], send_sem=sem_v.at[0], recv_sem=sem_v.at[1],
+            device_id=(a, nth_lev(i)), device_id_type=MESH,
+        ).start()
+
+    @pl.loop(1, SETS)
+    def _(i):
+        pltpu.make_async_remote_copy(
+            src_ref=wave_me, dst_ref=wave_set.at[a], send_sem=sem_w1.at[0], recv_sem=sem_w1.at[1],
+            device_id=(nth_set(i), b), device_id_type=MESH,
+        ).start()
+
+    for p in range(1, PAIRS):
+        load(p)
 
     sub = iota((8, 128), 0)
     cv = jnp.zeros((8, 128), F32)
@@ -114,11 +125,11 @@
     clane[0:1, :] = clane_row
     clane[1:2, :] = 1.0 / clane_row
     cinv[...] = 1.0 / cv
-    for t in range(LONS // 128):
+    for t in range(SPAN // 128):
         x = ((iota((8, 128), 1) + t * 128) * TRUNC).astype(F32)
         pc, ps = turn(x, cval[...], cinv[...])
-        psi_c[:, t * 128 : t * 128 + 128] = pc
-        psi_s[:, t * 128 : t * 128 + 128] = ps
+        psi_c[t] = pc
+        psi_s[t] = ps
 
     @pl.loop(0, 8)
     def _(i):
@@ -142,41 +153,27 @@
         axis=1,
     ).astype(BF16)
 
-    @pl.loop(0, PAIRS)
-    def _(p):
+    for f in range(2):
+        for p in range(PAIRS):
+            sbuf[f, p, 2576 : 2 * PAD] = jnp.zeros((2 * PAD - 2576, 128), BF16)
+
+    def turn_tables(p):
         for c in load_tables(p):
             c.wait()
 
-        @pl.loop(0, 5)
-        def _(t):
-            j0 = pl.multiple_of(t * 256, 256)
-            both = jnp.concatenate([tbuf[0, p, pl.ds(j0, 256)], tbuf[1, p, pl.ds(j0, 256)]], axis=1)
+        for t in range(5):
+            j0 = 256 * t
+            both = jnp.concatenate([tbuf[0, p, j0 : j0 + 256], tbuf[1, p, j0 : j0 + 256]], axis=1)
             turned = lax.dot_general(order, both, (((1,), (1,)), ((), ())), preferred_element_type=F32)
-            tpt[p, :, pl.ds(j0, 256)] = turned.astype(BF16)
+            tpt[:, j0 : j0 + 256] = turned.astype(BF16)
 
         last = jnp.concatenate([tbuf[0, p, 1280:1281], tbuf[1, p, 1280:1281]], axis=1).astype(F32)
         last = jnp.broadcast_to(last, (128, 256))
         last = jnp.where(iota((128, 256), 0) == 0, last, 0.0).astype(BF16)
         turned = lax.dot_general(order, last, (((1,), (1,)), ((), ())), preferred_element_type=F32)
-        tpt[p, :, 1280:PAD] = turned.astype(BF16)
-
-    own_v.wait()
-    pl.semaphore_wait(bar, LEVS - 1 + SETS - 1)
-
-    @pl.loop(1, LEVS)
-    def _(i):
-        pltpu.make_async_remote_copy(
-            src_ref=vall.at[b], dst_ref=vall.at[b], send_sem=sem_v.at[0], recv_sem=sem_v.at[1],
-            device_id=(a, nth_lev(i)), device_id_type=MESH,
-        ).start()
-
-    @pl.loop(1, SETS)
-    def _(i):
-        pltpu.make_async_remote_copy(
-            src_ref=wave_me, dst_ref=wave_set.at[a], send_sem=sem_w1.at[0], recv_sem=sem_w1.at[1],
-            device_id=(nth_set(i), b), device_id_type=MESH,
-        ).start()
-
+        tpt[:, 1280:PAD] = turned.astype(BF16)
+
+    turn_tables(0)
     for e in range(2):
         pltpu.make_async_copy(vall.at[pl.ds(0, LEVS - 1)], vall.at[pl.ds(0, LEVS - 1)], sem_v.at[e]).wait()
     for f in range(2):
@@ -220,8 +217,7 @@
     def send1(p):
         local(p, 0).start()
 
-        @pl.loop(1, SETS)
-        def _(i):
+        for i in range(1, SETS):
             t = nth_set(i)
             pltpu.make_async_remote_copy(
                 src_ref=xbuf.at[p, t, 0], dst_ref=ra.at[p, a], send_sem=sem_a1.at[0, p], recv_sem=sem_a1.at[1, p],
@@ -250,8 +246,7 @@
             wait_bytes(rb.at[p, pl.ds(0, LEVS - 1)], sem_b1.at[1, p])
             local(p, 3).start()
 
-            @pl.loop(1, SETS)
-            def _(i):
+            for i in range(1, SETS):
                 t = nth_set(i)
                 pltpu.make_async_remote_copy(
                     src_ref=rb.at[p, :, t], dst_ref=dbuf.at[p, :, a],
@@ -282,6 +277,10 @@
         m = wave[p]
         for c in load_spec(p):
             c.wait()
+        @pl.when(p == 0)
+        def _():
+            load_ends.wait()
+
         for f in range(2):
             end = slast[f, p].reshape(2, 128).astype(F32)
             sbuf[f, p, 2560:2576] = jnp.concatenate([end, jnp.zeros((14, 128), F32)], axis=0).astype(BF16)
@@ -303,15 +302,15 @@
 
         w_low = jnp.where(m == 0, 1.0, 2.0)
         jl = iota((256, HIGH0), 1) + HIGH0
-        edge = tpt[p, :, HIGH0:1280].astype(F32)
+        edge = tpt[:, HIGH0:1280].astype(F32)
         low_hi = jnp.where(jl <= TRUNC - m, edge * w_low, 0.0).astype(BF16)
         low = jnp.dot(
-            (tpt[p, :, 0:HIGH0].astype(F32) * w_low).astype(BF16), abuf[0:HIGH0, :], preferred_element_type=F32
+            (tpt[:, 0:HIGH0].astype(F32) * w_low).astype(BF16), abuf[0:HIGH0, :], preferred_element_type=F32
         )
         low = low + jnp.dot(low_hi, abuf[HIGH0:1280, :], preferred_element_type=F32)
         jh = iota((256, PAD - HIGH0), 1) + HIGH0
         keep = jnp.logical_and(jh > TRUNC - m, jh < ROWS)
-        high_t = jnp.where(keep, tpt[p, :, HIGH0:PAD].astype(F32) * 2.0, 0.0).astype(BF16)
+        high_t = jnp.where(keep, tpt[:, HIGH0:PAD].astype(F32) * 2.0, 0.0).astype(BF16)
         high = jnp.dot(high_t, abuf[HIGH0:PAD, :], preferred_element_type=F32)
         band = jnp.concatenate([low.astype(BF16), high.astype(BF16)], axis=1)
         for q in range(4):
@@ -342,7 +341,11 @@
         legendre(p)
         send1(p)
 
-        @pl.when(p == 0)
+        @pl.when(p < PAIRS - 1)
+        def _():
+            turn_tables(p + 1)
+
+        @pl.when(p == 1)
         def _():
             pass_waves()
 
@@ -364,9 +367,11 @@
         wcol[...] = m_all
         sc, sn = turn(m_all * 128.0, clane[0:1, :], clane[1:2, :])
         m_row = jnp.broadcast_to(wave_t[pl.ds(p, 1), :], (8, 128))
-        shift_c, shift_s = turn(m_row * SPAN, cval[...], cinv[...])
-        shift[p, 0] = shift_c
-        shift[p, 1] = shift_s
+        for h, waves_h in enumerate((m_row, TRUNC - m_row)):
+            for t in range(1, LONS // SPAN):
+                shift_c, shift_s = turn(waves_h * (SPAN * t), cval[...], cinv[...])
+                shift[p, h, t, 0] = shift_c
+                shift[p, h, t, 1] = shift_s
         step[0] = sc
         step[1] = sn
 
@@ -374,7 +379,7 @@
         def _(s):
             count = cval[pl.ds(s, 1), :]
             inverse = cinv[pl.ds(s, 1), :]
-            row = pl.multiple_of(p * 256, 256)
+            row = pl.multiple_of(p * 512, 512)
             pick_s = iota((32, 128), 1) == s
             for g in range(4):
                 rows = slice(32 * g, 32 * g + 32)
@@ -386,8 +391,11 @@
                     for e in range(2)
                 )
                 for t in range(SPAN // 128):
-                    table[s, pl.ds(row + 32 * g, 32), 128 * t : 128 * t + 128] = c.astype(BF16)
-                    table[s, pl.ds(row + 128 + 32 * g, 32), 128 * t : 128 * t + 128] = n.astype(BF16)
+                    cols = slice(128 * t, 128 * t + 128)
+                    pc = psi_c[t, pl.ds(s, 1), :]
+                    ps = psi_s[t, pl.ds(s, 1), :]
+                    for e, v in enumerate((c, n, pc * c + ps * n, ps * c - pc * n)):
+                        table[s, pl.ds(row + 128 * e + 32 * g, 32), cols] = v.astype(BF16)
                     if t < SPAN // 128 - 1:
                         c, n = c * sc - n * sn, n * sc + c * sn
 
@@ -397,23 +405,22 @@
 
         @pl.loop(0, SLOTS)
         def _(s):
-            tc = shift[p, 0, pl.ds(s, 1), :]
-            ts = shift[p, 1, pl.ds(s, 1), :]
-            c0 = pl.multiple_of(p * 256, 256)
-            c1 = pl.multiple_of(c0 + 128, 128)
+            c0 = pl.multiple_of(p * 512, 512)
             for k in range(2):
                 x = df[pl.ds(k * 8 + s, 128, stride=16), :].T
-                re0, im0, re1, im1 = x[0:32], x[32:64], x[64:96], x[96:128]
-                for t in range(2):
-                    if t == 1:
-                        re0, im0 = re0 * tc - im0 * ts, re0 * ts + im0 * tc
-                        re1, im1 = re1 * tc + im1 * ts, im1 * tc - re1 * ts
-                    for g, (v, w) in enumerate(((re0, -im0), (re1, im1), (-im1, re1))):
-                        row = 192 * t + 64 * g + 32 * k
-                        lhs[s, row : row + 32, pl.ds(c0, 128)] = v.astype(BF16)
-                        lhs[s, row : row + 32, pl.ds(c1, 128)] = w.astype(BF16)
-
-    FIRST = 256 * (PAIRS - 1)
+                for t in range(LONS // SPAN):
+                    for h in range(2):
+                        re, im = x[64 * h : 64 * h + 32], x[64 * h + 32 : 64 * h + 64]
+                        if t > 0:
+                            tc = shift[p, h, t, 0, pl.ds(s, 1), :]
+                            ts = shift[p, h, t, 1, pl.ds(s, 1), :]
+                            re, im = re * tc - im * ts, re * ts + im * tc
+                        row = 64 * t + 32 * k
+                        for e, v in enumerate((re, -im)):
+                            at = pl.multiple_of(c0 + 256 * h + 128 * e, 128)
+                            lhs[s, row : row + 32, pl.ds(at, 128)] = v.astype(BF16)
+
+    FIRST = 512 * (PAIRS - 1)
 
     @pl.loop(0, PAIRS)
     def _(p):
@@ -431,30 +438,21 @@
 
     @pl.loop(0, SLOTS)
     def _(s):
-        for t in range(SPAN // 256):
-            cols = slice(256 * t, 256 * t + 256)
-            acc[s, :, cols] = jnp.dot(lhs[s, :, 0:FIRST], table[s, 0:FIRST, cols], preferred_element_type=F32)
+        acc[s] = jnp.dot(lhs[s, :, 0:FIRST], table[s, 0:FIRST, :], preferred_element_type=F32)
 
     gather(4)
 
     @pl.loop(0, SLOTS)
     def _(s):
         count = jnp.concatenate([cval[pl.ds(s, 1), :]] * 2, axis=1)
-        for t in range(SPAN // 256):
-            cols = slice(256 * t, 256 * t + 256)
-            total = acc[s, :, cols] + jnp.dot(
-                lhs[s, :, FIRST : 256 * PAIRS], table[s, FIRST : 256 * PAIRS, cols], preferred_element_type=F32
-            )
-            for u in range(2):
-                first = SPAN * u + 256 * t
-                pc = psi_c[pl.ds(s, 1), first : first + 256]
-                ps = psi_s[pl.ds(s, 1), first : first + 256]
-                r = 192 * u
-                o = total[r : r + 64] + pc * total[r + 64 : r + 128] + ps * total[r + 128 : r + 192]
-                lon = (iota((64, 256), 1) + first).astype(F32)
-                o = jnp.where(lon < count, o, 0.0)
-                for e in range(2):
-                    outf[first // 128 + e, pl.ds(s, 64, stride=8), :] = o[:, 128 * e : 128 * e + 128]
+        total = acc[s] + jnp.dot(
+            lhs[s, :, FIRST : 512 * PAIRS], table[s, FIRST : 512 * PAIRS, :], preferred_element_type=F32
+        )
+        for t in range(LONS // SPAN):
+            lon = (iota((64, 256), 1) + SPAN * t).astype(F32)
+            o = jnp.where(lon < count, total[64 * t : 64 * t + 64], 0.0)
+            for e in range(2):
+                outf[2 * t + e, pl.ds(s, 64, stride=8), :] = o[:, 128 * e : 128 * e + 128]
 
     for t in range(8):
         outb[:, :, :, :, 128 * t : 128 * t + 128] = outf[t].reshape(2, 2, 16, 8, 128).astype(BF16)
@@ -473,13 +471,33 @@
         c.wait()
 
 
+def hand_over(in_f, in_s, out_f, out_s, held, sems):
+    parts = [(n, f, h) for n in range(2) for f in range(2) for h in range(2)]
+
+    def come(n, f, h):
+        src = (in_f, in_s)[n].at[f, pl.ds(8 * h, 8)]
+        return pltpu.make_async_copy(src, held.at[n, f, pl.ds(8 * h, 8)], sems.at[0, n, f, h])
+
+    def go(n, f, h):
+        dst = (out_f, out_s)[n].at[f, pl.ds(8 * h, 8)]
+        return pltpu.make_async_copy(held.at[n, f, pl.ds(8 * h, 8)], dst, sems.at[1, n, f, h])
+
+    for part in parts:
+        come(*part).start()
+    for part in parts:
+        come(*part).wait()
+        go(*part).start()
+    for part in parts:
+        go(*part).wait()
+
+
 def body(spectral, vertical, value_table, slope_table, wave_low, lat_slot, lon_counts):
     rows_first = jnp.transpose(spectral, (0, 3, 4, 2, 1))
     anywhere = pl.BlockSpec(memory_space=pl.ANY)
     scalars = pl.BlockSpec(memory_space=pltpu.SMEM)
     dma = pltpu.SemaphoreType.DMA
     out = jax.ShapeDtypeStruct((2, 16, SLOTS, LONS), BF16)
-    return pl.pallas_call(
+    gridded = pl.pallas_call(
         kernel,
         out_shape=(out, out),
         in_specs=[anywhere] * 4 + [scalars] * 3 + [pl.BlockSpec(memory_space=pltpu.VMEM)],
@@ -488,7 +506,7 @@
             pltpu.VMEM((2, PAIRS, 2 * PAD, 128), BF16),
             pltpu.VMEM((2, PAIRS, 1, 2, 128), BF16),
             pltpu.VMEM((2, PAIRS, ROWS, 128), BF16),
-            pltpu.VMEM((PAIRS, 256, PAD), BF16),
+            pltpu.VMEM((256, PAD), BF16),
             pltpu.VMEM((1024, 1024), BF16),
             pltpu.VMEM((PAD, 512), BF16),
             pltpu.VMEM((2, 2 * BLK, 128), F32),
@@ -504,20 +522,20 @@
             pltpu.VMEM((LEVS, SETS, 128), F32),
             pltpu.VMEM((128, 128), F32),
             pltpu.VMEM((128, 128), F32),
-            pltpu.VMEM((PAIRS, 2, 8, 128), F32),
+            pltpu.VMEM((PAIRS, 2, LONS // SPAN, 2, 8, 128), F32),
             pltpu.VMEM((2, 128, 128), F32),
             pltpu.VMEM((8, 128), F32),
             pltpu.VMEM((8, 128), F32),
             pltpu.VMEM((8, 128), F32),
-            pltpu.VMEM((8, LONS), F32),
-            pltpu.VMEM((8, LONS), F32),
-            pltpu.VMEM((SLOTS, PAIRS * 256, SPAN), BF16),
-            pltpu.VMEM((SLOTS, 384, PAIRS * 256), BF16),
-            pltpu.VMEM((SLOTS, 384, SPAN), F32),
+            pltpu.VMEM((SPAN // 128, 8, 128), F32),
+            pltpu.VMEM((SPAN // 128, 8, 128), F32),
+            pltpu.VMEM((SLOTS, PAIRS * 512, SPAN), BF16),
+            pltpu.VMEM((SLOTS, 256, PAIRS * 512), BF16),
+            pltpu.VMEM((SLOTS, 256, SPAN), F32),
             pltpu.VMEM((2048, 128), F32),
             pltpu.VMEM((8, 512, 128), F32),
             pltpu.VMEM((2, 2, 16, SLOTS, LONS), BF16),
-            dma((4, PAIRS)),
+            dma((3, PAIRS)),
             dma((2, PAIRS)),
             dma((3,)),
             dma((2,)),
@@ -536,6 +554,13 @@
         rows_first, vertical, value_table, slope_table, wave_low, lat_slot, lon_counts,
         lat_slot.reshape(1, 128),
     )
+    return pl.pallas_call(
+        hand_over,
+        out_shape=(out, out),
+        in_specs=[anywhere] * 2,
+        out_specs=(anywhere, anywhere),
+        scratch_shapes=[pltpu.VMEM((2, 2, 16, SLOTS, LONS), BF16), dma((2, 2, 2, 2))],
+    )(*gridded)
 
 
 def solution(mesh):

time: 69.1 us -> 60.3 us (0.87)
  Pallas kernels: 64.5 us -> 59.5 us
  local copies, waits for them, and re-layouts: 3.74 us -> 0 us
    pallas_call x1, Pallas kernels: 64.5 us -> 57.4 us  [body(): pl.pallas_call(kernel, out_shape=(out, out), in_specs=[anywhere] * 4 + [s...]
    unnamed x2 -> x0, local copies, waits for them, and re-layouts: 3.74 us -> none
    pallas_call x0 -> x1, Pallas kernels: none -> 2.09 us  [body(): pl.pallas_call(hand_over, out_shape=(out, out), in_specs=[anywhere] * 2,...]
where the time goes in v3:
time: 60.3 us; the launch traced here: 60.1 us
  Pallas kernels  59.5 us (99%)
  between operations  0.64 us (1%)
    pallas_call x1, Pallas kernels, body(): pl.pallas_call(kernel, out_shape=(out, out), in_specs=[anywhere] * 4 + [s...  57.4 us
    pallas_call x1, Pallas kernels, body(): pl.pallas_call(hand_over, out_shape=(out, out), in_specs=[anywhere] * 2,...  2.09 us

profile of v3, /device:TPU:1, one launch (start us, length us, event | category | flops | bytes accessed | tf_op | source)
XLA Modules:
  0.0 60.1 jit_solution(17714342889333052642)
XLA Ops:
  0.6 57.4 %shard_map.86 = (bf16[2,16,8,1024]{3,2,1,0:T(8,128)(2,1)}, bf16[2,16,8,1024]{3,2,1,0:T(8,128)(2,1)}) custom-call(bf16[2,5,1281,2,128]{4,3,2,1,0:T(2,128)(2,1)} %bitcast.2, bf16[2,16,128]{2,1,0:T(8,128)(2,1)} %vert.1, bf16[5,1281,128]{2,1,0:T(8,128)(2,1)} %tabs_v.1, bf16[5,1281,128]{2,1,0:T(8,128)(2,1)} %tabs_s.1, s32[5]{0:T(128)} %wave.1, s32[128]{0:T(128)} %lat.1, ...), custom_call_target="tpu_custom_call" | custom-call | tf_op jit(solution)/shard_map/pallas_call | solution.py:500
  58.0 2.1 %shard_map.87 = (bf16[2,16,8,1024]{3,2,1,0:T(8,128)(2,1)}, bf16[2,16,8,1024]{3,2,1,0:T(8,128)(2,1)}) custom-call(bf16[2,16,8,1024]{3,2,1,0:T(8,128)(2,1)} %get-tuple-element.4.in_f, bf16[2,16,8,1024]{3,2,1,0:T(8,128)(2,1)} %get-tuple-element.5.in_s), custom_call_target="tpu_custom_call" | custom-call | tf_op jit(solution)/shard_map/pallas_call | solution.py:557

commit v4 on v3

--- a/solution.py
+++ b/solution.py
@@ -285,7 +285,7 @@
             end = slast[f, p].reshape(2, 128).astype(F32)
             sbuf[f, p, 2560:2576] = jnp.concatenate([end, jnp.zeros((14, 128), F32)], axis=0).astype(BF16)
 
-        @pl.loop(0, PAD // BLK)
+        @pl.loop(0, PAD // BLK, unroll=2)
         def _(t):
             j0 = pl.multiple_of(t * BLK, BLK)
             j = iota((2 * BLK, 128), 0) // 2 + j0
@@ -403,7 +403,7 @@
         wait2(p)
         df[...] = dbuf[p].reshape(2048, 128).astype(F32)
 
-        @pl.loop(0, SLOTS)
+        @pl.loop(0, SLOTS, unroll=4)
         def _(s):
             c0 = pl.multiple_of(p * 512, 512)
             for k in range(2):
@@ -436,13 +436,13 @@
 
     gather(3)
 
-    @pl.loop(0, SLOTS)
+    @pl.loop(0, SLOTS, unroll=4)
     def _(s):
         acc[s] = jnp.dot(lhs[s, :, 0:FIRST], table[s, 0:FIRST, :], preferred_element_type=F32)
 
     gather(4)
 
-    @pl.loop(0, SLOTS)
+    @pl.loop(0, SLOTS, unroll=4)
     def _(s):
         count = jnp.concatenate([cval[pl.ds(s, 1), :]] * 2, axis=1)
         total = acc[s] + jnp.dot(

time: 60.3 us -> 55.8 us (0.925)
  Pallas kernels: 59.5 us -> 55 us
    pallas_call x1, Pallas kernels: 57.4 us -> 52.9 us  [body(): pl.pallas_call(kernel, out_shape=(out, out), in_specs=[anywhere] * 4 + [s...]
where the time goes in v4:
time: 55.8 us; the launch traced here: 55.6 us
  Pallas kernels  55 us (99%)
  between operations  0.64 us (1%)
    pallas_call x1, Pallas kernels, body(): pl.pallas_call(kernel, out_shape=(out, out), in_specs=[anywhere] * 4 + [s...  52.9 us
    pallas_call x1, Pallas kernels, body(): pl.pallas_call(hand_over, out_shape=(out, out), in_specs=[anywhere] * 2,...  2.09 us

profile of v4, /device:TPU:1, one launch (start us, length us, event | category | flops | bytes accessed | tf_op | source)
XLA Modules:
  0.0 55.6 jit_solution(13612601904475173858)
XLA Ops:
  0.6 52.9 %shard_map.86 = (bf16[2,16,8,1024]{3,2,1,0:T(8,128)(2,1)}, bf16[2,16,8,1024]{3,2,1,0:T(8,128)(2,1)}) custom-call(bf16[2,5,1281,2,128]{4,3,2,1,0:T(2,128)(2,1)} %bitcast.2, bf16[2,16,128]{2,1,0:T(8,128)(2,1)} %vert.1, bf16[5,1281,128]{2,1,0:T(8,128)(2,1)} %tabs_v.1, bf16[5,1281,128]{2,1,0:T(8,128)(2,1)} %tabs_s.1, s32[5]{0:T(128)} %wave.1, s32[128]{0:T(128)} %lat.1, ...), custom_call_target="tpu_custom_call" | custom-call | tf_op jit(solution)/shard_map/pallas_call | solution.py:500
  53.5 2.1 %shard_map.87 = (bf16[2,16,8,1024]{3,2,1,0:T(8,128)(2,1)}, bf16[2,16,8,1024]{3,2,1,0:T(8,128)(2,1)}) custom-call(bf16[2,16,8,1024]{3,2,1,0:T(8,128)(2,1)} %get-tuple-element.4.in_f, bf16[2,16,8,1024]{3,2,1,0:T(8,128)(2,1)} %get-tuple-element.5.in_s), custom_call_target="tpu_custom_call" | custom-call | tf_op jit(solution)/shard_map/pallas_call | solution.py:557

commit v5 on v4

--- a/solution.py
+++ b/solution.py
@@ -375,7 +375,7 @@
         step[0] = sc
         step[1] = sn
 
-        @pl.loop(0, SLOTS)
+        @pl.loop(0, SLOTS, unroll=2)
         def _(s):
             count = cval[pl.ds(s, 1), :]
             inverse = cinv[pl.ds(s, 1), :]

time: 55.8 us -> 55.4 us (level)
  no operation moved by 1% of the time
where the time goes in v5:
time: 55.4 us; the launch traced here: 55.2 us
  Pallas kernels  54.6 us (99%)
  between operations  0.64 us (1%)
    pallas_call x1, Pallas kernels, body(): pl.pallas_call(kernel, out_shape=(out, out), in_specs=[anywhere] * 4 + [s...  52.5 us
    pallas_call x1, Pallas kernels, body(): pl.pallas_call(hand_over, out_shape=(out, out), in_specs=[anywhere] * 2,...  2.09 us

profile of v5, /device:TPU:1, one launch (start us, length us, event | category | flops | bytes accessed | tf_op | source)
XLA Modules:
  0.0 55.2 jit_solution(17317117561616264980)
XLA Ops:
  0.6 52.5 %shard_map.86 = (bf16[2,16,8,1024]{3,2,1,0:T(8,128)(2,1)}, bf16[2,16,8,1024]{3,2,1,0:T(8,128)(2,1)}) custom-call(bf16[2,5,1281,2,128]{4,3,2,1,0:T(2,128)(2,1)} %bitcast.2, bf16[2,16,128]{2,1,0:T(8,128)(2,1)} %vert.1, bf16[5,1281,128]{2,1,0:T(8,128)(2,1)} %tabs_v.1, bf16[5,1281,128]{2,1,0:T(8,128)(2,1)} %tabs_s.1, s32[5]{0:T(128)} %wave.1, s32[128]{0:T(128)} %lat.1, ...), custom_call_target="tpu_custom_call" | custom-call | tf_op jit(solution)/shard_map/pallas_call | solution.py:500
  53.1 2.1 %shard_map.87 = (bf16[2,16,8,1024]{3,2,1,0:T(8,128)(2,1)}, bf16[2,16,8,1024]{3,2,1,0:T(8,128)(2,1)}) custom-call(bf16[2,16,8,1024]{3,2,1,0:T(8,128)(2,1)} %get-tuple-element.4.in_f, bf16[2,16,8,1024]{3,2,1,0:T(8,128)(2,1)} %get-tuple-element.5.in_s), custom_call_target="tpu_custom_call" | custom-call | tf_op jit(solution)/shard_map/pallas_call | solution.py:557
